TPU v7x, 256 devices: a whole 4x4x8 slice. The times are simulated.
256 devices in a mesh: rep: 32 (over x_hi, z, core), head: 8 (over x_lo, y).
Axes of the slice: x: 4 (x_hi: 2, x_lo: 2; x = x_hi * 2 + x_lo), y: 4, z: 8, core: 2. Of those that a mesh axis runs over, the one named last changes fastest.
Arguments:
- queries: bfloat16 [4096, 32, 128], P('rep', 'head'), may hold values from -6 to 6
- tree_keys: bfloat16 [4096, 8, 128], P('rep', 'head'), may hold values from -160 to 160
- tree_values: bfloat16 [4096, 8, 128], P('rep', 'head'), may hold values from -6 to 6
- prefix_keys: bfloat16 [128, 8, 128, 128], P('rep', 'head'), may hold values from -6 to 6
- prefix_values: bfloat16 [128, 8, 128, 128], P('rep', 'head'), may hold values from -6 to 6
- tree_parent: int32 [4096], P('rep'), may hold values from 0 to 62, as said below
- page_table: int32 [64, 16], P('rep'), may hold values from 0 to 127, all different within a row
- out_weight: bfloat16 [4096, 5120], P('head'), may hold values from -1.5 to 1.5
Outputs:
- mixed: bfloat16 [4096, 5120], P(('rep', 'head'))
Inputs may be any that keep to these rules, and one draw needn't show every extreme that they name: `tree_parent`: within each session a row's parent is an earlier row, the first row being its own parent. `page_table`: each session names 16 different pages; every page is named by some session.
All inputs are finite; a program needn't handle non-finite values.
Results may differ from a plain program's by a relative error of at most 0.019.
Values may be sent and summed in bfloat16 or wider, within the bound.
No kernel may reach another device: no remote copies, remote signals or barrier semaphores. Data moves between devices by JAX's collectives and lax.ppermute only.
A program may use at most 64 MiB of HBM per device.

v0:
```python
import jax
import jax.numpy as jnp
from jax import lax
from jax.sharding import PartitionSpec as P


def ancestors(parent):
    count = parent.shape[0]
    onehot = (parent[:, None] == jnp.arange(count, dtype=jnp.int32)[None, :]).astype(jnp.float32)
    reach = jnp.eye(count, dtype=jnp.float32) + onehot
    for level in range(count.bit_length()):
        reach = jnp.minimum(jnp.dot(reach, reach, precision=lax.Precision.HIGHEST), 1.0)
    return reach > 0.5


def on_device(
    queries, tree_keys, tree_values, prefix_keys, prefix_values, tree_parent, page_table, out_weight
):
    rows, qh_dev, head_size = queries.shape
    kvh_dev = tree_keys.shape[1]
    group = qh_dev // kvh_dev
    sess_dev = page_table.shape[0]
    used = page_table.shape[1]
    tree = rows // sess_dev
    page = prefix_keys.shape[2]
    scale = head_size ** (-0.5)
    visible = jax.vmap(ancestors)(tree_parent.reshape(sess_dev, tree))
    q_sess = queries.reshape(sess_dev, tree, kvh_dev, group, head_size)
    k_sess = tree_keys.reshape(sess_dev, tree, kvh_dev, head_size)
    v_sess = tree_values.reshape(sess_dev, tree, kvh_dev, head_size)
    s_tree = (
        jnp.einsum("stkgd,sukd->kgstu", q_sess, k_sess, preferred_element_type=jnp.float32) * scale
    )
    s_tree = jnp.where(visible[None, None], s_tree, -1e30)
    all_keys, all_vals = (
        lax.all_gather(prefix_keys, "rep", axis=0, tiled=True),
        lax.all_gather(prefix_values, "rep", axis=0, tiled=True),
    )
    flat_ids = page_table.reshape(sess_dev * used)
    sel_keys = jnp.take(all_keys, flat_ids, axis=0).reshape(
        sess_dev, used, kvh_dev, page, head_size
    )
    sel_vals = jnp.take(all_vals, flat_ids, axis=0).reshape(
        sess_dev, used, kvh_dev, page, head_size
    )
    sel_keys = sel_keys.transpose(0, 2, 1, 3, 4).reshape(sess_dev, kvh_dev, used * page, head_size)
    sel_vals = sel_vals.transpose(0, 2, 1, 3, 4).reshape(sess_dev, kvh_dev, used * page, head_size)
    s_pre = (
        jnp.einsum("stkgd,skpd->kgstp", q_sess, sel_keys, preferred_element_type=jnp.float32)
        * scale
    )
    top = jnp.maximum(jnp.max(s_pre, axis=-1), jnp.max(s_tree, axis=-1))
    e_pre = jnp.exp(s_pre - top[..., None])
    e_tree = jnp.exp(s_tree - top[..., None])
    total = jnp.sum(e_pre, axis=-1) + jnp.sum(e_tree, axis=-1)
    numer = jnp.einsum(
        "kgstp,skpd->kgstd",
        e_pre.astype(jnp.bfloat16),
        sel_vals,
        preferred_element_type=jnp.float32,
    )
    numer = numer + jnp.einsum(
        "kgstu,sukd->kgstd", e_tree.astype(jnp.bfloat16), v_sess, preferred_element_type=jnp.float32
    )
    state = (
        top.reshape(kvh_dev, group, rows),
        total.reshape(kvh_dev, group, rows),
        numer.reshape(kvh_dev, group, rows, head_size),
    )
    top, total, acc = state
    attn = (acc / total[..., None]).astype(jnp.bfloat16)
    attn = attn.transpose(2, 0, 1, 3).reshape(rows, qh_dev * head_size)
    return lax.psum_scatter(
        jnp.dot(attn, out_weight, preferred_element_type=jnp.float32).astype(jnp.bfloat16),
        "head",
        scatter_dimension=0,
        tiled=True,
    )


def solution(mesh):
    in_specs = (
        P("rep", "head", None),
        P("rep", "head", None),
        P("rep", "head", None),
        P("rep", "head", None, None),
        P("rep", "head", None, None),
        P("rep"),
        P("rep", None),
        P("head", None),
    )
    out_specs = P(("rep", "head"), None)
    return jax.shard_map(
        on_device, mesh=mesh, in_specs=in_specs, out_specs=out_specs, check_vma=False
    )
```

profile of v0, /device:TPU:2, one launch (start us, length us, event | category | flops | bytes accessed | tf_op | source)
XLA Modules:
  0.0 241.9 jit_solution(13033656732809941557)
XLA Ops:
  6.5 0.7 all-gather.3.cloned.1.call-update
  7.3 0.7 all-gather.5.cloned.1.call-update
  8.1 0.8 reshape.127
  8.8 0.7 eq.23
  9.6 0.3 convolution_minimum_fusion.6
  9.8 0.2 convolution_minimum_fusion.5
  10.0 0.2 convolution_minimum_fusion.4
  10.2 0.2 convolution_minimum_fusion.3
  10.4 0.2 convolution_minimum_fusion.2
  10.6 0.2 convolution_minimum_fusion.1
  10.8 0.2 fusion.12
  11.2 1.0 fusion.28
  12.2 86.8 %all-gather.3.cloned.1.call-done = bf16[128,1,128,128]{3,2,1,0:T(8,128)(2,1)} async-done(((bf16[4,1,128,128]{3,2,1,0:T(8,128)(2,1)}), bf16[128,1,128,128]{3,2,1,0:T(8,128)(2,1)}) %all-gather.3.cloned.1.call-update) | async-done | bytes 4194320 | tf_op jit(solution)/shard_map/all_gather | solution.py:37
  99.1 2.9 %gather_fusion = bf16[32,128,128]{2,1,0:T(8,128)(2,1)S(1)} fusion(bf16[128,128,128]{2,1,0:T(8,128)(2,1)} %bitcast.93, s32[1024]{0:T(1024)S(1)} %pad_clamp_fusion), kind=kCustom, calls=%fused_computation.clone | custom fusion | bytes 2097280 | tf_op jit(solution)/shard_map/jit(_take)/gather | solution.py:43
  102.0 83.4 %all-gather.5.cloned.1.call-done = bf16[128,1,128,128]{3,2,1,0:T(8,128)(2,1)} async-done(((bf16[4,1,128,128]{3,2,1,0:T(8,128)(2,1)}), bf16[128,1,128,128]{3,2,1,0:T(8,128)(2,1)}) %all-gather.5.cloned.1.call-update) | async-done | bytes 4194320 | tf_op jit(solution)/shard_map/all_gather | solution.py:36
  185.4 2.9 %gather_fusion.1 = bf16[32,128,128]{2,1,0:T(8,128)(2,1)S(1)} fusion(bf16[128,128,128]{2,1,0:T(8,128)(2,1)} %bitcast.94, s32[1024]{0:T(1024)S(1)} %pad_clamp_fusion), kind=kCustom, calls=%fused_computation.1.clone | custom fusion | bytes 2097280 | tf_op jit(solution)/shard_map/jit(_take)/gather | solution.py:40
  188.3 0.3 bitcast_select_fusion
  188.6 0.8 bitcast_reduce_fusion
  189.4 0.8 fusion.1
  190.2 0.8 fusion.4
  191.1 0.2 fusion.10
  191.5 0.1 fusion.13
  191.8 4.4 %convolution_convert_fusion = bf16[128,5120]{1,0:T(8,128)(2,1)} fusion(bf16[128,512]{0,1:T(8,128)(2,1)S(1)} %bitcast.92, bf16[512,5120]{1,0:T(8,128)(2,1)} %param.17), kind=kOutput, calls=%fused_computation.2 | convolution fusion | flops 671744000 | bytes 6684672 | tf_op jit(solution)/shard_map/dot_general | solution.py:74
  196.3 39.1 %reduce-scatter.2.cloned.1.call-done = bf16[16,5120]{1,0:T(8,128)(2,1)} async-done(((bf16[128,5120]{1,0:T(8,128)(2,1)}), bf16[16,5120]{1,0:T(8,128)(2,1)}) %reduce-scatter.2.cloned.1.call-update) | async-done | bytes 163856 | tf_op jit(solution)/shard_map/reduce_scatter | solution.py:73
  (20 shorter events, 0.5 us)
Async XLA Ops:
  6.5 4.7 %copy-start = (bf16[128,4,128]{2,1,0:T(4,128)(2,1)S(1)}, bf16[128,4,128]{2,1,0:T(4,128)(2,1)}, u32[]{:S(2)}) copy-start(bf16[128,4,128]{2,1,0:T(4,128)(2,1)} %param.10) | copy-start | bytes 393220
  6.5 92.5 %all-gather.3.cloned.1.call-start = ((), (), s32[]{:S(2)}) async-start(), calls=%async_computation.1 | async-start | bytes 4325376 | tf_op jit(solution)/shard_map/all_gather | solution.py:37
  7.3 178.1 %all-gather.5.cloned.1.call-start = ((), (), s32[]{:S(2)}) async-start(), calls=%async_computation.2 | async-start | bytes 4325376 | tf_op jit(solution)/shard_map/all_gather | solution.py:36
  8.0 227.4 %reduce-scatter.2.cloned.1.call-start = ((), (), s32[]{:S(2)}) async-start(), calls=%async_computation.3 | async-start | bytes 1474560 | tf_op jit(solution)/shard_map/reduce_scatter | solution.py:73
  189.4 1.8 copy-start.1
Sparse Core Ops, SparseCore 0:
  10.1 88.8 all-gather.2
  101.8 83.4 all-gather.4
  196.4 38.9 reduce-scatter.1
where the time goes:
time: 243 us; the launch traced here: 242 us
  waiting for transfers between devices  211 us (87%)
  between operations  13.3 us (5%)
  matrix products  8.75 us (4%)
  local copies, waits for them, and re-layouts  7.71 us (3%)
    all_gather x1, waiting for transfers between devices, on_device(): lax.all_gather(prefix_values, 'rep', axis=0, tiled=True)  86.8 us
    all_gather x1, waiting for transfers between devices, on_device(): lax.all_gather(prefix_keys, 'rep', axis=0, tiled=True)  83.4 us
    reduce_scatter x1, waiting for transfers between devices, on_device(): lax.psum_scatter(jnp.dot(attn, out_weight, preferred_element_type=jnp.flo...  39.1 us
  transfers between devices with their start and end apart: 3, of which 3 were waited for; matrix products, arithmetic and copies ran while one was open for 3% of the time, Pallas kernels for 0%

commit v1 on v0

v1 whole, which is shorter than its diff:
```python
import functools
import math

import jax
import jax.numpy as jnp
from jax import lax
from jax.experimental import pallas as pl
from jax.experimental.pallas import tpu as pltpu
from jax.sharding import PartitionSpec as P

NEG = -1e30
Z = 8
GROUP = 4
LOCAL_PAGES = 4
TREE = 64
QROWS = 256
HD = 128
SESS = 8
C2 = (HD ** -0.5) * math.log2(math.e)
BF = jnp.bfloat16
F32 = jnp.float32

NEAR = (0, -1, 1, -2, 2)
FAR = (-3, 3, 4)


def rep_of(xh, z, c):
    return xh * 16 + (z % Z) * 2 + c


def z_perm(k):
    return [(rep_of(a, z, c), rep_of(a, z + k, c)) for a in range(2) for z in range(Z) for c in range(2)]


def group_perm(r):
    return [(rep_of(a, z, c), rep_of(a ^ (r >> 1), z, c ^ (r & 1))) for a in range(2) for z in range(Z) for c in range(2)]


def pair_step(entry, q_ref, kv, m_ref, l_ref, a_ref):
    s = entry >> 8
    k_at = entry & 255
    scores = lax.dot_general(kv[k_at], q_ref[s & (SESS - 1)], (((1,), (1,)), ((), ())), preferred_element_type=F32)
    old = m_ref[s]
    new = jnp.maximum(old, jnp.max(scores, axis=0, keepdims=True))
    probs = jnp.exp2(scores * C2 - new * C2)
    fix = jnp.exp2((old - new) * C2)
    m_ref[s] = new
    l_ref[s] = l_ref[s] * fix + jnp.sum(probs, axis=0, keepdims=True)
    part = lax.dot_general(kv[k_at + LOCAL_PAGES], probs.astype(BF), (((0,), (0,)), ((), ())), preferred_element_type=F32)
    a_ref[s] = a_ref[s] * fix + part


def all_pairs(count, entry_at, q_ref, kv, streams):
    @pl.loop(0, lax.shift_right_logical(count + 1, 1))
    def _(i):
        for r, (m_ref, l_ref, a_ref) in enumerate(streams):
            pair_step(entry_at(2 * i + r), q_ref, kv, m_ref, l_ref, a_ref)


def clear(streams):
    for m_ref, l_ref, a_ref in streams:
        m_ref[...] = jnp.full(m_ref.shape, NEG, F32)
        l_ref[...] = jnp.zeros(l_ref.shape, F32)
        a_ref[...] = jnp.zeros(a_ref.shape, F32)


def merge(states):
    top = functools.reduce(jnp.maximum, [m for m, _, _ in states])
    ws = [jnp.exp2((m - top) * C2) for m, _, _ in states]
    total = sum(w * l for w, (_, l, _) in zip(ws, states))
    acc = sum(w * a for w, (_, _, a) in zip(ws, states))
    return top, total, acc


def near_kernel(*refs):
    nb = len(NEAR)
    tbl, map_near, map_far, parent, tk, tv, q_ref = refs[:7]
    blocks = refs[7:7 + nb]
    list_far, m_out, l_out, a_out = refs[7 + nb:11 + nb]
    kv, m0, l0, a0, m1, l1, a1, list_near, sems = refs[11 + nb:]
    copies = [pltpu.make_async_copy(b, kv.at[pl.ds(i * 8, 8)], sems.at[i]) for i, b in enumerate(blocks)]
    for cp in copies:
        cp.start()
    clear(((m0, l0, a0), (m1, l1, a1)))

    def scan(s, counts):
        n, f = counts
        for j in range(16):
            page = tbl[s, j]
            owner = lax.shift_right_logical(page, 2)
            entry = s * 256 + (page & 3)
            near = map_near[owner]
            far = map_far[owner]
            list_near[n] = entry + near
            list_far[f + 1] = entry + far
            n = n + (near >= 0).astype(jnp.int32)
            f = f + (far >= 0).astype(jnp.int32)
        return n, f

    n, f = lax.fori_loop(0, SESS, scan, (jnp.int32(0), jnp.int32(0)))
    list_near[n] = jnp.int32(SESS * 256)
    list_far[f + 1] = jnp.int32(SESS * 256)
    list_far[0] = f

    lane = lax.broadcasted_iota(jnp.int32, (TREE, TREE), 1)
    eye = (lax.broadcasted_iota(jnp.int32, (TREE, TREE), 0) == lane).astype(F32)
    widen = (
        lax.broadcasted_iota(jnp.int32, (TREE, QROWS), 0)
        == lax.shift_right_logical(lax.broadcasted_iota(jnp.int32, (TREE, QROWS), 1), 2)
    ).astype(BF)
    for s in range(2):
        rows = pl.ds(s * TREE, TREE)
        reach = jnp.minimum(eye + (parent[rows, :] == lane).astype(F32), 1.0)
        for _ in range(7):
            half = reach.astype(BF)
            reach = jnp.minimum(jnp.dot(half, half, preferred_element_type=F32), 1.0)
        seen = lax.dot_general(reach.astype(BF), widen, (((0,), (0,)), ((), ())), preferred_element_type=F32)
        scores = lax.dot_general(tk[rows, :], q_ref[s], (((1,), (1,)), ((), ())), preferred_element_type=F32)
        scores = jnp.where(seen > 0.5, scores, NEG)
        top = jnp.max(scores, axis=0, keepdims=True)
        probs = jnp.exp2(scores * C2 - top * C2)
        m0[s] = top
        l0[s] = jnp.sum(probs, axis=0, keepdims=True)
        a0[s] = lax.dot_general(tv[rows, :], probs.astype(BF), (((0,), (0,)), ((), ())), preferred_element_type=F32)

    for cp in copies:
        cp.wait()
    all_pairs(n, lambda i: list_near[i], q_ref, kv, ((m0, l0, a0), (m1, l1, a1)))
    for s in range(SESS):
        top, total, acc = merge(((m0[s], l0[s], a0[s]), (m1[s], l1[s], a1[s])))
        m_out[s] = top
        l_out[s] = total
        a_out[s] = acc


def far_kernel(*refs):
    nb = len(FAR)
    list_far, q_ref = refs[:2]
    blocks = refs[2:2 + nb]
    m_in, l_in, a_in = refs[2 + nb:5 + nb]
    own = refs[5 + nb]
    outs = refs[6 + nb:9 + nb]
    kv, m0, l0, a0, m1, l1, a1, sems = refs[9 + nb:]
    copies = [pltpu.make_async_copy(b, kv.at[pl.ds(i * 8, 8)], sems.at[i]) for i, b in enumerate(blocks)]
    for cp in copies:
        cp.start()
    clear(((m0, l0, a0), (m1, l1, a1)))
    for cp in copies:
        cp.wait()
    all_pairs(list_far[0], lambda i: list_far[i + 1], q_ref, kv, ((m0, l0, a0), (m1, l1, a1)))
    for s in range(SESS):
        top, total, acc = merge(
            ((m_in[s], l_in[s], a_in[s]), (m0[s], l0[s], a0[s]), (m1[s], l1[s], a1[s]))
        )
        some = total > 0.0
        safe = jnp.where(some, total, 1.0)
        acc = acc * (1.0 / safe)
        lse = jnp.where(some, top * C2 + jnp.log2(safe), NEG)
        lanes = pl.ds((s % 2) * QROWS, QROWS)
        if s < 2:
            own[pl.ds(0, HD), lanes] = acc
            own[pl.ds(HD, 8), lanes] = jnp.broadcast_to(lse, (8, QROWS))
        else:
            out = outs[s // 2 - 1]
            out[pl.ds(0, HD), lanes] = acc.astype(BF)
            hi = lse.astype(BF).astype(F32)
            mid = (lse - hi).astype(BF).astype(F32)
            low = lse - hi - mid
            row = lax.broadcasted_iota(jnp.int32, (16, QROWS), 0)
            parts = jnp.where(row == 0, hi, jnp.where(row == 1, mid, jnp.where(row == 2, low, 0.0)))
            out[pl.ds(HD, 16), lanes] = parts.astype(BF)


def project_kernel(head_ref, own, p1, p2, p3, w_ref, *refs):
    outs = refs[:8]
    rows_f32, attn = refs[8:]

    @pl.when(pl.program_id(0) == 0)
    def _():
        lses = [own[HD:HD + 1, :]]
        vals = [own[:HD, :]]
        for p in (p1, p2, p3):
            tail = p[HD:HD + 16, :].astype(F32)
            lses.append(tail[0:1] + tail[1:2] + tail[2:3])
            vals.append(p[:HD, :].astype(F32))
        top = functools.reduce(jnp.maximum, lses)
        ws = [jnp.exp2(x - top) for x in lses]
        inv = 1.0 / sum(ws)
        mixed = sum(v * (w * inv) for v, w in zip(vals, ws))
        rows_f32[...] = mixed.T
        for k in range(8):
            first = (head_ref[0] ^ k) * 64
            for h in range(4):
                block = rows_f32[pl.ds(first + h, 16, stride=4), :]
                attn[pl.ds(k * 16, 16), pl.ds(h * HD, HD)] = block.astype(BF)

    res = jnp.dot(attn[...], w_ref[...], preferred_element_type=F32).astype(BF)
    for k in range(8):
        outs[k][...] = res[k * 16:(k + 1) * 16]


VMEM = pl.BlockSpec(memory_space=pltpu.VMEM)
SMEM = pl.BlockSpec(memory_space=pltpu.SMEM)
ANY = pl.BlockSpec(memory_space=pl.ANY)


def stream_scratch():
    return [
        pltpu.VMEM((SESS + 1, 1, QROWS), F32),
        pltpu.VMEM((SESS + 1, 1, QROWS), F32),
        pltpu.VMEM((SESS + 1, HD, QROWS), F32),
    ]


def on_device(
    queries, tree_keys, tree_values, prefix_keys, prefix_values, tree_parent, page_table, out_weight
):
    rep = lax.axis_index("rep")
    head = lax.axis_index("head")
    kv = jnp.concatenate([prefix_keys, prefix_values], axis=0).reshape(8, 128, HD)
    up1 = lax.ppermute(kv, "rep", z_perm(1))
    dn1 = lax.ppermute(kv, "rep", z_perm(-1))
    up2 = lax.ppermute(kv, "rep", z_perm(2))
    dn2 = lax.ppermute(kv, "rep", z_perm(-2))
    q_own = queries.reshape(2 * QROWS, HD)
    table_rows = jnp.pad(page_table.reshape(1, 32).astype(BF), ((0, 15), (0, 96)))
    sent = jnp.concatenate([q_own, table_rows], axis=0)
    got = [lax.ppermute(sent, "rep", group_perm(r)) for r in (1, 2, 3)]
    q_all = jnp.concatenate([q_own] + [g[:2 * QROWS] for g in got], axis=0).reshape(SESS, QROWS, HD)
    tables = [page_table] + [g[2 * QROWS, :32].astype(jnp.int32).reshape(2, 16) for g in got]
    table = jnp.concatenate(tables, axis=0)
    up3 = lax.ppermute(up2, "rep", z_perm(1))
    dn3 = lax.ppermute(dn2, "rep", z_perm(-1))
    up4 = lax.ppermute(up2, "rep", z_perm(2))

    reps = jnp.arange(32, dtype=jnp.int32)
    same = ((reps ^ rep) & 17) == 0
    step = ((reps >> 1) - (rep >> 1)) & 7

    def place(offsets):
        at = jnp.full((32,), -100000, jnp.int32)
        for i, k in enumerate(offsets):
            at = jnp.where(same & (step == k % Z), i * 8, at)
        return at

    blocks_near = [kv, up1, dn1, up2, dn2]
    blocks_far = [up3, dn3, up4]
    nn, nf = len(NEAR), len(FAR)
    state = [
        jax.ShapeDtypeStruct((SESS, 1, QROWS), F32),
        jax.ShapeDtypeStruct((SESS, 1, QROWS), F32),
        jax.ShapeDtypeStruct((SESS, HD, QROWS), F32),
    ]
    list_far, m, l, a = pl.pallas_call(
        near_kernel,
        out_shape=[jax.ShapeDtypeStruct((160,), jnp.int32)] + state,
        in_specs=[SMEM] * 3 + [VMEM] * 4 + [ANY] * nn,
        out_specs=[SMEM, VMEM, VMEM, VMEM],
        scratch_shapes=[pltpu.VMEM((8 * nn, 128, HD), BF)]
        + stream_scratch()
        + stream_scratch()
        + [pltpu.SMEM((160,), jnp.int32), pltpu.SemaphoreType.DMA((nn,))],
        compiler_params=pltpu.CompilerParams(vmem_limit_bytes=24 << 20),
        cost_estimate=pl.CostEstimate(flops=4 * 10**9, bytes_accessed=4 << 20, transcendentals=1 << 20),
        name="near_pages",
    )(
        table, place(NEAR), place(FAR), tree_parent.reshape(-1, 1), tree_keys.reshape(-1, HD),
        tree_values.reshape(-1, HD), q_all, *blocks_near,
    )
    own, p1, p2, p3 = pl.pallas_call(
        far_kernel,
        out_shape=[jax.ShapeDtypeStruct((HD + 8, 2 * QROWS), F32)]
        + [jax.ShapeDtypeStruct((HD + 16, 2 * QROWS), BF)] * 3,
        in_specs=[SMEM, VMEM] + [ANY] * nf + [VMEM] * 3,
        out_specs=[VMEM] * 4,
        scratch_shapes=[pltpu.VMEM((8 * nf, 128, HD), BF)]
        + stream_scratch()
        + stream_scratch()
        + [pltpu.SemaphoreType.DMA((nf,))],
        compiler_params=pltpu.CompilerParams(vmem_limit_bytes=24 << 20),
        cost_estimate=pl.CostEstimate(flops=2 * 10**9, bytes_accessed=4 << 20, transcendentals=1 << 20),
        name="far_pages",
    )(list_far, q_all, *blocks_far, m, l, a)
    back = [lax.ppermute(p, "rep", group_perm(r)) for r, p in ((1, p1), (2, p2), (3, p3))]
    cols = 1024
    width = out_weight.shape[1]
    parts = pl.pallas_call(
        project_kernel,
        grid=(width // cols,),
        out_shape=[jax.ShapeDtypeStruct((16, width), BF)] * 8,
        in_specs=[SMEM]
        + [pl.BlockSpec((HD + 8, 2 * QROWS), lambda i: (0, 0))]
        + [pl.BlockSpec((HD + 16, 2 * QROWS), lambda i: (0, 0))] * 3
        + [pl.BlockSpec((512, cols), lambda i: (0, i))],
        out_specs=[pl.BlockSpec((16, cols), lambda i: (0, i))] * 8,
        scratch_shapes=[pltpu.VMEM((2 * QROWS, HD), F32), pltpu.VMEM((128, 512), BF)],
        compiler_params=pltpu.CompilerParams(vmem_limit_bytes=24 << 20),
        cost_estimate=pl.CostEstimate(flops=2 * 128 * 512 * width, bytes_accessed=8 << 20, transcendentals=4096),
        name="combine_project",
    )(head.reshape(1).astype(jnp.int32), own, *back, out_weight)
    total = parts[0].astype(F32)
    for k in (2, 6, 5, 7, 1, 3, 4):
        total = total + lax.ppermute(parts[k], "head", [(i, i ^ k) for i in range(8)]).astype(F32)
    return total.astype(BF)


def solution(mesh):
    in_specs = (
        P("rep", "head", None),
        P("rep", "head", None),
        P("rep", "head", None),
        P("rep", "head", None, None),
        P("rep", "head", None, None),
        P("rep"),
        P("rep", None),
        P("head", None),
    )
    out_specs = P(("rep", "head"), None)
    return jax.shard_map(
        on_device, mesh=mesh, in_specs=in_specs, out_specs=out_specs, check_vma=False
    )
```

time: 243 us -> 94.7 us (0.39)
  the two profiles are of different devices: /device:TPU:2 before, /device:TPU:32 now
where the time goes in v1:
time: 94.7 us; the launch traced here: 93.1 us
  starting transfers between devices  34.7 us (37%)
  waiting for transfers between devices  32.6 us (34%)
  Pallas kernels  15.4 us (16%)
  other arithmetic  5.13 us (5%)
  local copies, waits for them, and re-layouts  5.13 us (5%)
    ppermute x7, starting transfers between devices, on_device(): lax.ppermute(parts[k], 'head', [(i, i ^ k) for i in range(8)]).astype(F32)  14.3 us
    ppermute x7, waiting for transfers between devices, on_device(): lax.ppermute(parts[k], 'head', [(i, i ^ k) for i in range(8)]).astype(F32)  10.6 us
    pallas_call x1, Pallas kernels, on_device(): pl.pallas_call(near_kernel, out_shape=[jax.ShapeDtypeStruct((160,), jnp.i...  8.78 us
    ppermute x1, waiting for transfers between devices, on_device(): up2 = lax.ppermute(kv, 'rep', z_perm(2))  7.77 us
    ppermute x3, waiting for transfers between devices, on_device(): lax.ppermute(p, 'rep', group_perm(r))  7.27 us
    ppermute x1, waiting for transfers between devices, on_device(): up4 = lax.ppermute(up2, 'rep', z_perm(2))  5.78 us
    ppermute x1, starting transfers between devices, on_device(): up4 = lax.ppermute(up2, 'rep', z_perm(2))  4.59 us
    ppermute x3, starting transfers between devices, on_device(): lax.ppermute(p, 'rep', group_perm(r))  4.44 us
  transfers between devices with their start and end apart: 20, of which 8 were waited for; matrix products, arithmetic and copies ran while one was open for 4% of the time, Pallas kernels for 9%

profile of v1, /device:TPU:32, one launch (start us, length us, event | category | flops | bytes accessed | tf_op | source)
XLA Modules:
  0.0 93.1 jit_solution(7462512336255847908)
XLA Ops:
  1.8 3.1 %collective-permute-start.1 = (bf16[528,128]{1,0:T(8,128)(2,1)S(1)}, bf16[528,128]{1,0:T(8,128)(2,1)S(1)}, u32[]{:S(2)}, u32[]{:S(2)}) collective-permute-start(bf16[528,128]{1,0:T(8,128)(2,1)S(1)} %fusion.1), channel_id=1, source_target_pairs={{0,128},{8,136},{16,144},{24,152},{32,160},{40,168},{48,176},{56,1... | collective-permute-start | bytes 405512 | tf_op jit(solution)/shard_map/ppermute | solution.py:228
  5.2 1.0 %maximum_bitcast_fusion.refs_7_ = bf16[8,128,128]{2,1,0:T(8,128)(2,1)S(1)} fusion(bf16[4,1,128,128]{3,2,0,1:T(8,128)(2,1)} %bitcast.16, bf16[4,1,128,128]{3,2,0,1:T(8,128)(2,1)} %bitcast.17), kind=kLoop, calls=%fused_computation.4 | loop fusion | flops 131072 | bytes 524288 | tf_op jit(solution)/shard_map/reshape | solution.py:220
  6.2 3.4 %collective-permute-start.5 = (bf16[8,128,128]{2,1,0:T(8,128)(2,1)S(1)}, bf16[8,128,128]{2,1,0:T(8,128)(2,1)S(1)}, u32[]{:S(2)}, u32[]{:S(2)}) collective-permute-start(bf16[8,128,128]{2,1,0:T(8,128)(2,1)S(1)} %maximum_bitcast_fusion.refs_7_), channel_id=1, source_target_pairs={{0,32},{8,40},{16,48},{24,56},{32,64},{40,72},{48,80},{56,88},{64,... | collective-permute-start | bytes 786440 | tf_op jit(solution)/shard_map/ppermute | solution.py:223
  9.5 2.2 %collective-permute-start.6 = (bf16[8,128,128]{2,1,0:T(8,128)(2,1)S(1)}, bf16[8,128,128]{2,1,0:T(8,128)(2,1)S(1)}, u32[]{:S(2)}, u32[]{:S(2)}) collective-permute-start(bf16[8,128,128]{2,1,0:T(8,128)(2,1)S(1)} %maximum_bitcast_fusion.refs_7_), channel_id=1, source_target_pairs={{0,96},{8,104},{16,112},{24,120},{32,0},{40,8},{48,16},{56,24},{64... | collective-permute-start | bytes 786440 | tf_op jit(solution)/shard_map/ppermute | solution.py:224
  12.5 1.0 %collective-permute-start.3 = (bf16[8,128,128]{2,1,0:T(8,128)(2,1)S(1)}, bf16[8,128,128]{2,1,0:T(8,128)(2,1)S(1)}, u32[]{:S(2)}, u32[]{:S(2)}) collective-permute-start(bf16[8,128,128]{2,1,0:T(8,128)(2,1)S(1)} %maximum_bitcast_fusion.refs_7_), channel_id=1, source_target_pairs={{0,16},{8,24},{16,32},{24,40},{32,48},{40,56},{48,64},{56,72},{64,... | collective-permute-start | bytes 786440 | tf_op jit(solution)/shard_map/ppermute | solution.py:221
  13.6 1.1 %collective-permute-start.4 = (bf16[8,128,128]{2,1,0:T(8,128)(2,1)S(1)}, bf16[8,128,128]{2,1,0:T(8,128)(2,1)S(1)}, u32[]{:S(2)}, u32[]{:S(2)}) collective-permute-start(bf16[8,128,128]{2,1,0:T(8,128)(2,1)S(1)} %maximum_bitcast_fusion.refs_7_), channel_id=1, source_target_pairs={{0,112},{8,120},{16,0},{24,8},{32,16},{40,24},{48,32},{56,40},{64,... | collective-permute-start | bytes 786440 | tf_op jit(solution)/shard_map/ppermute | solution.py:222
  16.6 7.8 %collective-permute-done.5.refs_10_ = bf16[8,128,128]{2,1,0:T(8,128)(2,1)S(1)} collective-permute-done((bf16[8,128,128]{2,1,0:T(8,128)(2,1)S(1)}, bf16[8,128,128]{2,1,0:T(8,128)(2,1)S(1)}, u32[]{:S(2)}, u32[]{:S(2)}) %collective-permute-start.5) | collective-permute-done | bytes 262176 | tf_op jit(solution)/shard_map/ppermute | solution.py:223
  24.7 4.6 %collective-permute-start.9 = (bf16[8,128,128]{2,1,0:T(8,128)(2,1)S(1)}, bf16[8,128,128]{2,1,0:T(8,128)(2,1)S(1)}, u32[]{:S(2)}, u32[]{:S(2)}) collective-permute-start(bf16[8,128,128]{2,1,0:T(8,128)(2,1)S(1)} %collective-permute-done.5.refs_10_), channel_id=1, source_target_pairs={{0,32},{8,40},{16,48},{24,56},{32,64},{40,72},{48,80},{56,88},{64,... | collective-permute-start | bytes 786440 | tf_op jit(solution)/shard_map/ppermute | solution.py:234
  29.3 1.2 %collective-permute-done.4.refs_9_ = bf16[8,128,128]{2,1,0:T(8,128)(2,1)S(1)} collective-permute-done((bf16[8,128,128]{2,1,0:T(8,128)(2,1)S(1)}, bf16[8,128,128]{2,1,0:T(8,128)(2,1)S(1)}, u32[]{:S(2)}, u32[]{:S(2)}) %collective-permute-start.4) | collective-permute-done | bytes 262176 | tf_op jit(solution)/shard_map/ppermute | solution.py:222
  32.0 8.8 %near_pages.1 = (s32[160]{0:T(256)S(1)}, f32[8,1,256]{2,1,0:T(1,128)S(1)}, f32[8,1,256]{2,1,0:T(1,128)S(1)}, f32[8,128,256]{2,1,0:T(8,128)S(1)}) custom-call(s32[8,16]{1,0:T(8,128)S(1)} %pad_add_fusion.refs_0_, s32[32]{0:T(128)S(1)} %get-tuple-element.38.refs_1_, s32[32]{0:T(128)S(1)} %get-tuple-element.37.refs_2_, s32[128,1]{1,0:T(8,128)S(1)} %copy.11.refs_3_, ...), custom_call_target="tpu_custom_call" | custom-call | flops 4000000000 | bytes 4194304 | tf_op jit(solution)/shard_map/near_pages/pallas_call | solution.py:254
  40.8 5.8 %collective-permute-done.9.refs_4_ = bf16[8,128,128]{2,1,0:T(8,128)(2,1)S(1)} collective-permute-done((bf16[8,128,128]{2,1,0:T(8,128)(2,1)S(1)}, bf16[8,128,128]{2,1,0:T(8,128)(2,1)S(1)}, u32[]{:S(2)}, u32[]{:S(2)}) %collective-permute-start.9) | collective-permute-done | bytes 262176 | tf_op jit(solution)/shard_map/ppermute | solution.py:234
  46.6 4.1 %far_pages.1 = (f32[136,512]{1,0:T(8,128)S(1)}, bf16[144,512]{1,0:T(8,128)(2,1)S(1)}, bf16[144,512]{1,0:T(8,128)(2,1)S(1)}, bf16[144,512]{1,0:T(8,128)(2,1)S(1)}) custom-call(s32[160]{0:T(256)S(1)} %get-tuple-element.21.refs_0_, bf16[8,256,128]{2,1,0:T(8,128)(2,1)S(1)} %bitcast.11, bf16[8,128,128]{2,1,0:T(8,128)(2,1)S(1)} %collective-permute-done.7.refs_2_, ...), custom_call_target="tpu_custom_call" | custom-call | flops 2000000000 | bytes 4194304 | tf_op jit(solution)/shard_map/far_pages/pallas_call | solution.py:270
  50.8 4.3 %collective-permute-start.11 = (bf16[144,512]{1,0:T(8,128)(2,1)S(1)}, bf16[144,512]{1,0:T(8,128)(2,1)S(1)}, u32[]{:S(2)}, u32[]{:S(2)}) collective-permute-start(bf16[144,512]{1,0:T(8,128)(2,1)S(1)} %get-tuple-element.27), channel_id=1, source_target_pairs={{0,128},{8,136},{16,144},{24,152},{32,160},{40,168},{48,176},{56,1... | collective-permute-start | bytes 442376 | tf_op jit(solution)/shard_map/ppermute | solution.py:284
  55.1 4.4 %collective-permute-done.11.p2 = bf16[144,512]{1,0:T(8,128)(2,1)S(1)} collective-permute-done((bf16[144,512]{1,0:T(8,128)(2,1)S(1)}, bf16[144,512]{1,0:T(8,128)(2,1)S(1)}, u32[]{:S(2)}, u32[]{:S(2)}) %collective-permute-start.11) | collective-permute-done | bytes 147488 | tf_op jit(solution)/shard_map/ppermute | solution.py:284
  59.5 2.9 %collective-permute-done.12.p3 = bf16[144,512]{1,0:T(8,128)(2,1)S(1)} collective-permute-done((bf16[144,512]{1,0:T(8,128)(2,1)S(1)}, bf16[144,512]{1,0:T(8,128)(2,1)S(1)}, u32[]{:S(2)}, u32[]{:S(2)}) %collective-permute-start.12) | collective-permute-done | bytes 147488 | tf_op jit(solution)/shard_map/ppermute | solution.py:284
  62.4 2.5 %copy-done = bf16[512,5120]{1,0:T(8,128)(2,1)S(1)} copy-done((bf16[512,5120]{1,0:T(8,128)(2,1)S(1)}, bf16[512,5120]{1,0:T(8,128)(2,1)}, u32[]{:S(2)}) %copy-start) | copy-done | bytes 5242904
  64.9 2.5 %combine_project.1 = (bf16[16,5120]{1,0:T(8,128)(2,1)S(1)}, bf16[16,5120]{1,0:T(8,128)(2,1)S(1)}, bf16[16,5120]{1,0:T(8,128)(2,1)S(1)}, bf16[16,5120]{1,0:T(8,12...) custom-call(s32[1]{0:T(128)} %bitcast.head_ref, ...), custom_call_target="tpu_custom_call" | custom-call | flops 671088640 | bytes 8388608 | tf_op jit(solution)/shard_map/combine_project/pallas_call | solution.py:287
  67.4 3.5 %collective-permute-start.13 = (bf16[16,5120]{1,0:T(8,128)(2,1)S(1)}, bf16[16,5120]{1,0:T(8,128)(2,1)S(1)}, u32[]{:S(2)}, u32[]{:S(2)}) collective-permute-start(bf16[16,5120]{1,0:T(8,128)(2,1)S(1)} %get-tuple-element.30), channel_id=1, source_target_pairs={{0,2},{1,3},{2,0},{3,1},{4,6},{5,7},{6,4},{7,5},{8,10},{9,11},{10,... | collective-permute-start | bytes 491528 | tf_op jit(solution)/shard_map/ppermute | solution.py:303
  71.2 2.4 %collective-permute-start.15 = (bf16[16,5120]{1,0:T(8,128)(2,1)S(1)}, bf16[16,5120]{1,0:T(8,128)(2,1)S(1)}, u32[]{:S(2)}, u32[]{:S(2)}) collective-permute-start(bf16[16,5120]{1,0:T(8,128)(2,1)S(1)} %get-tuple-element.32), channel_id=1, source_target_pairs={{0,5},{1,4},{2,7},{3,6},{4,1},{5,0},{6,3},{7,2},{8,13},{9,12},{10,... | collective-permute-start | bytes 491528 | tf_op jit(solution)/shard_map/ppermute | solution.py:303
  73.7 2.2 %collective-permute-start.16 = (bf16[16,5120]{1,0:T(8,128)(2,1)S(1)}, bf16[16,5120]{1,0:T(8,128)(2,1)S(1)}, u32[]{:S(2)}, u32[]{:S(2)}) collective-permute-start(bf16[16,5120]{1,0:T(8,128)(2,1)S(1)} %get-tuple-element.33), channel_id=1, source_target_pairs={{0,7},{1,6},{2,5},{3,4},{4,3},{5,2},{6,1},{7,0},{8,15},{9,14},{10,... | collective-permute-start | bytes 491528 | tf_op jit(solution)/shard_map/ppermute | solution.py:303
  76.5 5.9 %collective-permute-done.13 = bf16[16,5120]{1,0:T(8,128)(2,1)S(1)} collective-permute-done((bf16[16,5120]{1,0:T(8,128)(2,1)S(1)}, bf16[16,5120]{1,0:T(8,128)(2,1)S(1)}, u32[]{:S(2)}, u32[]{:S(2)}) %collective-permute-start.13) | collective-permute-done | bytes 163872 | tf_op jit(solution)/shard_map/ppermute | solution.py:303
  82.4 4.5 %collective-permute-start.18 = (bf16[16,5120]{1,0:T(8,128)(2,1)S(1)}, bf16[16,5120]{1,0:T(8,128)(2,1)S(1)}, u32[]{:S(2)}, u32[]{:S(2)}) collective-permute-start(bf16[16,5120]{1,0:T(8,128)(2,1)S(1)} %get-tuple-element.35), channel_id=1, source_target_pairs={{0,3},{1,2},{2,1},{3,0},{4,7},{5,6},{6,5},{7,4},{8,11},{9,10},{10,... | collective-permute-start | bytes 491528 | tf_op jit(solution)/shard_map/ppermute | solution.py:303
  87.6 2.7 %collective-permute-done.18 = bf16[16,5120]{1,0:T(8,128)(2,1)S(1)} collective-permute-done((bf16[16,5120]{1,0:T(8,128)(2,1)S(1)}, bf16[16,5120]{1,0:T(8,128)(2,1)S(1)}, u32[]{:S(2)}, u32[]{:S(2)}) %collective-permute-start.18) | collective-permute-done | bytes 163872 | tf_op jit(solution)/shard_map/ppermute | solution.py:303
  90.2 2.0 %collective-permute-done.19 = bf16[16,5120]{1,0:T(8,128)(2,1)S(1)} collective-permute-done((bf16[16,5120]{1,0:T(8,128)(2,1)S(1)}, bf16[16,5120]{1,0:T(8,128)(2,1)S(1)}, u32[]{:S(2)}, u32[]{:S(2)}) %collective-permute-start.19) | collective-permute-done | bytes 163872 | tf_op jit(solution)/shard_map/ppermute | solution.py:303
  (43 shorter events, 9.2 us)
Async XLA Ops:
  1.7 10.8 %collective-permute-start = (bf16[528,128]{1,0:T(8,128)(2,1)S(1)}, bf16[528,128]{1,0:T(8,128)(2,1)S(1)}, u32[]{:S(2)}, u32[]{:S(2)}) collective-permute-start(bf16[528,128]{1,0:T(8,128)(2,1)S(1)} %fusion.1), channel_id=1, source_target_pairs={{0,8},{8,0},{16,24},{24,16},{32,40},{40,32},{48,56},{56,48},{64,72... | collective-permute-start | bytes 405512 | tf_op jit(solution)/shard_map/ppermute | solution.py:228
  1.8 11.8 %collective-permute-start.1 = (bf16[528,128]{1,0:T(8,128)(2,1)S(1)}, bf16[528,128]{1,0:T(8,128)(2,1)S(1)}, u32[]{:S(2)}, u32[]{:S(2)}) collective-permute-start(bf16[528,128]{1,0:T(8,128)(2,1)S(1)} %fusion.1), channel_id=1, source_target_pairs={{0,128},{8,136},{16,144},{24,152},{32,160},{40,168},{48,176},{56,1... | collective-permute-start | bytes 405512 | tf_op jit(solution)/shard_map/ppermute | solution.py:228
  4.9 10.0 %collective-permute-start.2 = (bf16[528,128]{1,0:T(8,128)(2,1)S(1)}, bf16[528,128]{1,0:T(8,128)(2,1)S(1)}, u32[]{:S(2)}, u32[]{:S(2)}) collective-permute-start(bf16[528,128]{1,0:T(8,128)(2,1)S(1)} %fusion.1), channel_id=1, source_target_pairs={{0,136},{8,128},{16,152},{24,144},{32,168},{40,160},{48,184},{56,1... | collective-permute-start | bytes 405512 | tf_op jit(solution)/shard_map/ppermute | solution.py:228
  6.2 18.3 %collective-permute-start.5 = (bf16[8,128,128]{2,1,0:T(8,128)(2,1)S(1)}, bf16[8,128,128]{2,1,0:T(8,128)(2,1)S(1)}, u32[]{:S(2)}, u32[]{:S(2)}) collective-permute-start(bf16[8,128,128]{2,1,0:T(8,128)(2,1)S(1)} %maximum_bitcast_fusion.refs_7_), channel_id=1, source_target_pairs={{0,32},{8,40},{16,48},{24,56},{32,64},{40,72},{48,80},{56,88},{64,... | collective-permute-start | bytes 786440 | tf_op jit(solution)/shard_map/ppermute | solution.py:223
  9.5 19.8 %collective-permute-start.6 = (bf16[8,128,128]{2,1,0:T(8,128)(2,1)S(1)}, bf16[8,128,128]{2,1,0:T(8,128)(2,1)S(1)}, u32[]{:S(2)}, u32[]{:S(2)}) collective-permute-start(bf16[8,128,128]{2,1,0:T(8,128)(2,1)S(1)} %maximum_bitcast_fusion.refs_7_), channel_id=1, source_target_pairs={{0,96},{8,104},{16,112},{24,120},{32,0},{40,8},{48,16},{56,24},{64... | collective-permute-start | bytes 786440 | tf_op jit(solution)/shard_map/ppermute | solution.py:224
  12.5 16.8 %collective-permute-start.3 = (bf16[8,128,128]{2,1,0:T(8,128)(2,1)S(1)}, bf16[8,128,128]{2,1,0:T(8,128)(2,1)S(1)}, u32[]{:S(2)}, u32[]{:S(2)}) collective-permute-start(bf16[8,128,128]{2,1,0:T(8,128)(2,1)S(1)} %maximum_bitcast_fusion.refs_7_), channel_id=1, source_target_pairs={{0,16},{8,24},{16,32},{24,40},{32,48},{40,56},{48,64},{56,72},{64,... | collective-permute-start | bytes 786440 | tf_op jit(solution)/shard_map/ppermute | solution.py:221
  13.6 16.8 %collective-permute-start.4 = (bf16[8,128,128]{2,1,0:T(8,128)(2,1)S(1)}, bf16[8,128,128]{2,1,0:T(8,128)(2,1)S(1)}, u32[]{:S(2)}, u32[]{:S(2)}) collective-permute-start(bf16[8,128,128]{2,1,0:T(8,128)(2,1)S(1)} %maximum_bitcast_fusion.refs_7_), channel_id=1, source_target_pairs={{0,112},{8,120},{16,0},{24,8},{32,16},{40,24},{48,32},{56,40},{64,... | collective-permute-start | bytes 786440 | tf_op jit(solution)/shard_map/ppermute | solution.py:222
  24.4 16.4 %collective-permute-start.7 = (bf16[8,128,128]{2,1,0:T(8,128)(2,1)S(1)}, bf16[8,128,128]{2,1,0:T(8,128)(2,1)S(1)}, u32[]{:S(2)}, u32[]{:S(2)}) collective-permute-start(bf16[8,128,128]{2,1,0:T(8,128)(2,1)S(1)} %collective-permute-done.5.refs_10_), channel_id=1, source_target_pairs={{0,16},{8,24},{16,32},{24,40},{32,48},{40,56},{48,64},{56,72},{64,... | collective-permute-start | bytes 786440 | tf_op jit(solution)/shard_map/ppermute | solution.py:232
  24.7 21.9 %collective-permute-start.9 = (bf16[8,128,128]{2,1,0:T(8,128)(2,1)S(1)}, bf16[8,128,128]{2,1,0:T(8,128)(2,1)S(1)}, u32[]{:S(2)}, u32[]{:S(2)}) collective-permute-start(bf16[8,128,128]{2,1,0:T(8,128)(2,1)S(1)} %collective-permute-done.5.refs_10_), channel_id=1, source_target_pairs={{0,32},{8,40},{16,48},{24,56},{32,64},{40,72},{48,80},{56,88},{64,... | collective-permute-start | bytes 786440 | tf_op jit(solution)/shard_map/ppermute | solution.py:234
  29.3 17.3 %collective-permute-start.8 = (bf16[8,128,128]{2,1,0:T(8,128)(2,1)S(1)}, bf16[8,128,128]{2,1,0:T(8,128)(2,1)S(1)}, u32[]{:S(2)}, u32[]{:S(2)}) collective-permute-start(bf16[8,128,128]{2,1,0:T(8,128)(2,1)S(1)} %collective-permute-done.6.refs_11_), channel_id=1, source_target_pairs={{0,112},{8,120},{16,0},{24,8},{32,16},{40,24},{48,32},{56,40},{64,... | collective-permute-start | bytes 786440 | tf_op jit(solution)/shard_map/ppermute | solution.py:233
  30.5 0.8 copy-start.1
  31.2 0.8 copy-start.2
  50.7 4.5 %collective-permute-start.10 = (bf16[144,512]{1,0:T(8,128)(2,1)S(1)}, bf16[144,512]{1,0:T(8,128)(2,1)S(1)}, u32[]{:S(2)}, u32[]{:S(2)}) collective-permute-start(bf16[144,512]{1,0:T(8,128)(2,1)S(1)} %get-tuple-element.26), channel_id=1, source_target_pairs={{0,8},{8,0},{16,24},{24,16},{32,40},{40,32},{48,56},{56,48},{64,72... | collective-permute-start | bytes 442376 | tf_op jit(solution)/shard_map/ppermute | solution.py:284
  50.8 8.7 %collective-permute-start.11 = (bf16[144,512]{1,0:T(8,128)(2,1)S(1)}, bf16[144,512]{1,0:T(8,128)(2,1)S(1)}, u32[]{:S(2)}, u32[]{:S(2)}) collective-permute-start(bf16[144,512]{1,0:T(8,128)(2,1)S(1)} %get-tuple-element.27), channel_id=1, source_target_pairs={{0,128},{8,136},{16,144},{24,152},{32,160},{40,168},{48,176},{56,1... | collective-permute-start | bytes 442376 | tf_op jit(solution)/shard_map/ppermute | solution.py:284
  55.1 7.3 %collective-permute-start.12 = (bf16[144,512]{1,0:T(8,128)(2,1)S(1)}, bf16[144,512]{1,0:T(8,128)(2,1)S(1)}, u32[]{:S(2)}, u32[]{:S(2)}) collective-permute-start(bf16[144,512]{1,0:T(8,128)(2,1)S(1)} %get-tuple-element.28), channel_id=1, source_target_pairs={{0,136},{8,128},{16,152},{24,144},{32,168},{40,160},{48,184},{56,1... | collective-permute-start | bytes 442376 | tf_op jit(solution)/shard_map/ppermute | solution.py:284
  62.4 2.5 %copy-start = (bf16[512,5120]{1,0:T(8,128)(2,1)S(1)}, bf16[512,5120]{1,0:T(8,128)(2,1)}, u32[]{:S(2)}) copy-start(bf16[512,5120]{1,0:T(8,128)(2,1)} %w_ref.1) | copy-start | bytes 15728644
  67.4 15.1 %collective-permute-start.13 = (bf16[16,5120]{1,0:T(8,128)(2,1)S(1)}, bf16[16,5120]{1,0:T(8,128)(2,1)S(1)}, u32[]{:S(2)}, u32[]{:S(2)}) collective-permute-start(bf16[16,5120]{1,0:T(8,128)(2,1)S(1)} %get-tuple-element.30), channel_id=1, source_target_pairs={{0,2},{1,3},{2,0},{3,1},{4,6},{5,7},{6,4},{7,5},{8,10},{9,11},{10,... | collective-permute-start | bytes 491528 | tf_op jit(solution)/shard_map/ppermute | solution.py:303
  70.8 16.1 %collective-permute-start.14 = (bf16[16,5120]{1,0:T(8,128)(2,1)S(1)}, bf16[16,5120]{1,0:T(8,128)(2,1)S(1)}, u32[]{:S(2)}, u32[]{:S(2)}) collective-permute-start(bf16[16,5120]{1,0:T(8,128)(2,1)S(1)} %get-tuple-element.31), channel_id=1, source_target_pairs={{0,6},{1,7},{2,4},{3,5},{4,2},{5,3},{6,0},{7,1},{8,14},{9,15},{10,... | collective-permute-start | bytes 491528 | tf_op jit(solution)/shard_map/ppermute | solution.py:303
  71.2 16.3 %collective-permute-start.15 = (bf16[16,5120]{1,0:T(8,128)(2,1)S(1)}, bf16[16,5120]{1,0:T(8,128)(2,1)S(1)}, u32[]{:S(2)}, u32[]{:S(2)}) collective-permute-start(bf16[16,5120]{1,0:T(8,128)(2,1)S(1)} %get-tuple-element.32), channel_id=1, source_target_pairs={{0,5},{1,4},{2,7},{3,6},{4,1},{5,0},{6,3},{7,2},{8,13},{9,12},{10,... | collective-permute-start | bytes 491528 | tf_op jit(solution)/shard_map/ppermute | solution.py:303
  73.7 13.9 %collective-permute-start.16 = (bf16[16,5120]{1,0:T(8,128)(2,1)S(1)}, bf16[16,5120]{1,0:T(8,128)(2,1)S(1)}, u32[]{:S(2)}, u32[]{:S(2)}) collective-permute-start(bf16[16,5120]{1,0:T(8,128)(2,1)S(1)} %get-tuple-element.33), channel_id=1, source_target_pairs={{0,7},{1,6},{2,5},{3,4},{4,3},{5,2},{6,1},{7,0},{8,15},{9,14},{10,... | collective-permute-start | bytes 491528 | tf_op jit(solution)/shard_map/ppermute | solution.py:303
  75.9 11.7 %collective-permute-start.17 = (bf16[16,5120]{1,0:T(8,128)(2,1)S(1)}, bf16[16,5120]{1,0:T(8,128)(2,1)S(1)}, u32[]{:S(2)}, u32[]{:S(2)}) collective-permute-start(bf16[16,5120]{1,0:T(8,128)(2,1)S(1)} %get-tuple-element.34), channel_id=1, source_target_pairs={{0,1},{1,0},{2,3},{3,2},{4,5},{5,4},{6,7},{7,6},{8,9},{9,8},{10,11... | collective-permute-start | bytes 491528 | tf_op jit(solution)/shard_map/ppermute | solution.py:303
  82.4 7.8 %collective-permute-start.18 = (bf16[16,5120]{1,0:T(8,128)(2,1)S(1)}, bf16[16,5120]{1,0:T(8,128)(2,1)S(1)}, u32[]{:S(2)}, u32[]{:S(2)}) collective-permute-start(bf16[16,5120]{1,0:T(8,128)(2,1)S(1)} %get-tuple-element.35), channel_id=1, source_target_pairs={{0,3},{1,2},{2,1},{3,0},{4,7},{5,6},{6,5},{7,4},{8,11},{9,10},{10,... | collective-permute-start | bytes 491528 | tf_op jit(solution)/shard_map/ppermute | solution.py:303
  87.0 5.3 %collective-permute-start.19 = (bf16[16,5120]{1,0:T(8,128)(2,1)S(1)}, bf16[16,5120]{1,0:T(8,128)(2,1)S(1)}, u32[]{:S(2)}, u32[]{:S(2)}) collective-permute-start(bf16[16,5120]{1,0:T(8,128)(2,1)S(1)} %get-tuple-element.36), channel_id=1, source_target_pairs={{0,4},{1,5},{2,6},{3,7},{4,0},{5,1},{6,2},{7,3},{8,12},{9,13},{10,... | collective-permute-start | bytes 491528 | tf_op jit(solution)/shard_map/ppermute | solution.py:303
